TPU v7x, 32 devices: a whole 2x2x4 slice. The times are simulated.
32 devices in a mesh: grp: 2 (over y), frm: 4 (over z), row: 4 (over x, core).
Axes of the slice: x: 2, y: 2, z: 4, core: 2. Of those that a mesh axis runs over, the one named last changes fastest.
Arguments:
- queries: bfloat16 [16, 8, 128, 2240], P(('grp', 'frm'), 'row'), parts along dimension 0, may hold values from -6 to 6
- keys: bfloat16 [16, 8, 128, 2240], P(('grp', 'frm'), 'row'), parts along dimension 0, may hold values from -6 to 6
- values: bfloat16 [16, 8, 128, 2240], P(('grp', 'frm'), 'row'), parts along dimension 0, may hold values from -6 to 6
- flags: int32 [16], P(('grp', 'frm')), parts along dimension 0, may hold values 0 or 1
- blocks: int32 [16], P(('grp', 'frm')), parts along dimension 0, may hold values from 0 to 2, as said below
- out_weight: bfloat16 [2240, 2240], P('frm'), may hold values from -0.125 to 0.125
- norm_gain: float32 [2240], replicated, may hold values from 0.1 to 1.9
Outputs:
- projected: bfloat16 [16, 8, 128, 2240], P(('grp', 'frm'), 'row'), parts along dimension 0
There are 2 independent parts, one for each index of `grp`. A program takes and returns all parts, laid end to end along the dimension named above; an argument that names none is the same for every part. Nothing has to cross between parts.
Inputs may be any that keep to these rules, and one draw needn't show every extreme that they name: `flags`: 1 marks a clean frame, 0 a noisy one. `blocks`: within the 8 frames of one group, block numbers never fall and each block is 1 to 4 consecutive frames, some block exactly 4; every number from 0 to 2 occurs.
All inputs are finite; a program needn't handle non-finite values. No bound on the sum of `flags` on one device may be relied on, other than what follows from the above.
Results may differ from a plain program's by a relative error of at most 0.0049.
Values may be sent and summed in bfloat16 or wider, within the bound.
A program may use at most 192 MiB of HBM per device.

v0:
```python
import jax
import jax.numpy as jnp
from jax import lax
from jax.sharding import PartitionSpec as P

HEADS = 20
HD = 112


norm_eps = 1e-06


def entering(part, axis, combine, identity):
    place = lax.axis_index(axis)
    gathered = jax.tree.map(lambda a: lax.all_gather(a, axis), part)
    state = jax.tree.map(lambda a, e: jnp.zeros_like(a) + jnp.asarray(e, a.dtype), part, identity)

    def one(step, state):
        return combine(
            state, jax.tree.map(lambda a: lax.dynamic_index_in_dim(a, step, 0, False), gathered)
        )

    return lax.fori_loop(0, place, one, state)


def combine(earlier, later):
    closed_a, opened_a, latest_a = earlier
    closed_b, opened_b, latest_b = later
    advance = (latest_a < latest_b).astype(jnp.float32)
    return (
        closed_a + closed_b + advance * opened_a,
        opened_b + (1.0 - advance) * opened_a,
        jnp.maximum(latest_a, latest_b),
    )


def empty_carry(length):
    return (
        jnp.zeros((length,), jnp.float32),
        jnp.zeros((length,), jnp.float32),
        jnp.full((1,), -1.0, jnp.float32),
    )


def frame_element(frame_states, flag_values, block_values, frame_idx):
    length = frame_states.shape[1]
    return (
        jnp.zeros((length,), jnp.float32),
        flag_values[frame_idx] * frame_states[frame_idx],
        block_values[frame_idx : frame_idx + 1],
    )


def fold_frames(frame_states, flag_values, block_values):
    running = empty_carry(frame_states.shape[1])
    for frame_idx in range(frame_states.shape[0]):
        running = combine(
            running, frame_element(frame_states, flag_values, block_values, frame_idx)
        )
    return running


def read_frames(prefix, frame_states, flag_values, block_values):
    running = prefix
    collected = []
    for frame_idx in range(frame_states.shape[0]):
        advance = (running[2] < block_values[frame_idx : frame_idx + 1]).astype(jnp.float32)
        select = jnp.maximum(advance, flag_values[frame_idx])
        collected.append(running[0] + select * running[1] + frame_states[frame_idx])
        running = combine(
            running, frame_element(frame_states, flag_values, block_values, frame_idx)
        )
    return jnp.stack(collected)


def local(queries, keys, values, flags, blocks, out_weight, norm_gain):
    frames, lat_rows, lat_cols, model_width = queries.shape
    tokens = lat_rows * lat_cols
    key_pos = jax.nn.relu(keys).reshape(frames, tokens, HEADS, HD)
    value_heads = values.reshape(frames, tokens, HEADS, HD)
    partial_value = jnp.einsum(
        "ftha,fthb->fhab", key_pos, value_heads, preferred_element_type=jnp.float32
    )
    partial_value = partial_value.reshape(frames, HEADS * HD * HD)
    flag_values = flags.astype(jnp.float32)
    block_values = blocks.astype(jnp.float32)
    summed = lax.psum(partial_value, "row")
    totals = fold_frames(summed, flag_values, block_values)
    prefix = entering(
        (totals[0], totals[1], totals[2]), "frm", combine, empty_carry(summed.shape[1])
    )
    read_states = read_frames(prefix, summed, flag_values, block_values)
    read_tensor = read_states.reshape(frames, HEADS, HD, HD)
    query_pos = jax.nn.relu(queries).reshape(frames, tokens, HEADS, HD).astype(jnp.float32)
    attended = jnp.einsum(
        "ftha,fhab->fthb", query_pos, read_tensor, precision=lax.Precision.HIGHEST
    )
    inv_rms = lax.rsqrt(jnp.mean(attended * attended, axis=-1, keepdims=True) + norm_eps)
    gain_table = norm_gain.reshape(HEADS, HD)
    normed = (
        (attended * inv_rms * gain_table).astype(jnp.bfloat16).reshape(frames * tokens, model_width)
    )
    projected = jnp.dot(
        normed,
        lax.all_gather(out_weight, "frm", axis=0, tiled=True),
        preferred_element_type=jnp.float32,
    )
    return projected.astype(jnp.bfloat16).reshape(frames, lat_rows, lat_cols, model_width)


def solution(mesh):
    in_specs = (
        P(("grp", "frm"), "row", None, None),
        P(("grp", "frm"), "row", None, None),
        P(("grp", "frm"), "row", None, None),
        P(("grp", "frm")),
        P(("grp", "frm")),
        P("frm", None),
        P(),
    )
    out_specs = P(("grp", "frm"), "row", None, None)
    return jax.shard_map(local, mesh=mesh, in_specs=in_specs, out_specs=out_specs, check_vma=False)
```

profile of v0, /device:TPU:25, one launch (start us, length us, event | category | flops | bytes accessed | tf_op | source)
XLA Modules:
  0.0 472.4 jit_solution(3732474962754750551)
XLA Ops:
  6.5 0.0 all-reduce.3.cloned.1.call-start
  6.5 1.8 broadcast_maximum_fusion.1
  8.3 10.3 %copy.16 = bf16[2,2,128,2240]{2,1,3,0:T(2,128)(2,1)} copy(bf16[2,2,128,2240]{2,3,1,0:T(8,128)(2,1)S(1)} %broadcast_maximum_fusion.1) | data formatting | bytes 4587520 | tf_op jit(solution)/shard_map/jit(relu)/max | solution.py:79
  18.7 5.2 %reshape.37 = bf16[2,256,20,112]{1,3,2,0:T(8,128)(2,1)S(1)} reshape(bf16[2,2,128,2240]{2,1,3,0:T(2,128)(2,1)} %copy.16) | data formatting | bytes 4587520 | tf_op jit(solution)/shard_map/reshape | solution.py:79
  23.9 12.6 %copy.17 = bf16[2,2,128,2240]{2,1,3,0:T(2,128)(2,1)} copy(bf16[2,2,128,2240]{2,3,1,0:T(8,128)(2,1)} %param.11) | data formatting | bytes 4587520 | tf_op args[2]
  36.5 6.2 %reshape.38 = bf16[2,256,20,112]{1,3,2,0:T(8,128)(2,1)} reshape(bf16[2,2,128,2240]{2,1,3,0:T(2,128)(2,1)} %copy.17) | data formatting | bytes 4587520 | tf_op jit(solution)/shard_map/reshape | solution.py:80
  42.7 3.8 fusion.10
  46.5 0.0 copy-start.3
  46.5 0.0 copy-start.5
  46.5 5.6 %reshape.39 = f32[2,250880]{1,0:T(2,128)} reshape(f32[2,20,112,112]{3,2,1,0:T(8,128)} %fusion.10) | data formatting | bytes 4014080 | tf_op jit(solution)/shard_map/reshape | solution.py:84
  52.0 0.0 all-reduce.3.cloned.1.call-update
  52.0 0.0 all-gather.11.cloned.1.call-start
  52.1 0.0 copy-done.3
  52.1 0.0 copy-done.5
  52.1 0.6 dynamic-slice
  52.7 1.3 maximum_dynamic-update-slice_fusion
  55.9 0.0 copy-done.4
  55.9 0.6 fusion.9
  56.6 46.9 %all-reduce.3.cloned.1.call-done = f32[2,250880]{1,0:T(2,128)} async-done(((f32[2,250880]{1,0:T(2,128)}), f32[2,250880]{1,0:T(2,128)}) %all-reduce.3.cloned.1.call-update) | async-done | bytes 2007056 | tf_op jit(solution)/shard_map/psum | solution.py:87
  103.4 8.0 %fusion.8 = (f32[1,250880]{1,0:T(1,128)S(1)}, f32[1,1,250880]{2,1,0:T(1,128)}, f32[1,1,250880]{2,1,0:T(1,128)}, f32[1,250880]{1,0:T(1,128)}) fusion(f32[2,250880]{1,0:T(2,128)} %all-reduce.3.cloned.1.call-done, f32[]{:T(128)} %bitcast.7, f32[]{:T(128)} %bitcast.6, f32[]{:T(128)} %bitcast.5, f32[]{:T(128)} %bitcast.12, f32[]{:T(128)} %bitcast.11), kind=kLoop, calls=%fused_computation.27 | loop fusion | flops 1505280 | bytes 6021140 | tf_op jit(solution)/shard_map/slice | solution.py:49
  111.4 0.0 all-gather.11.cloned.1.call-update
  111.4 0.0 all-gather.9.cloned.1.call-start
  111.5 0.7 all-gather.9.cloned.1.call-update
  112.1 0.0 all-gather.7.cloned.1.call-start
  112.2 0.5 all-gather.7.cloned.1.call-update
  112.7 6.4 %all-reduce = f32[4]{0:T(128)S(1)} all-reduce(f32[4]{0:T(128)S(1)} %get-tuple-element.81), channel_id=2, replica_groups=mesh['grp'=2,'frm'=4,'row'=4] {'frm'}, use_global_device_ids=true, to_apply=%add | all-reduce | flops 4 | bytes 32
  119.1 0.0 copy-done.1
  119.1 0.1 broadcast_maximum_fusion
  119.3 10.1 %copy.20 = bf16[2,2,128,2240]{2,1,3,0:T(2,128)(2,1)S(1)} copy(bf16[2,2,128,2240]{2,3,1,0:T(8,128)(2,1)S(1)} %broadcast_maximum_fusion) | data formatting | bytes 4587520 | tf_op jit(solution)/shard_map/jit(relu)/max | solution.py:94
  129.3 0.0 copy-start.2
  129.4 2.7 reshape.40
  132.1 0.0 copy-done.2
  132.1 0.1 mul.175
  132.2 54.7 %all-gather.11.cloned.1.call-done = f32[4,1,250880]{2,1,0:T(1,128)} async-done(((f32[1,1,250880]{2,1,0:T(1,128)}), f32[4,1,250880]{2,1,0:T(1,128)}) %all-gather.11.cloned.1.call-update) | async-done | bytes 4014096 | tf_op jit(solution)/shard_map/all_gather | solution.py:15
  186.9 5.5 %copy.28 = f32[4,1,250880]{2,0,1:T(4,128)} copy(f32[4,1,250880]{2,1,0:T(1,128)} %all-gather.11.cloned.1.call-done) | data formatting | bytes 8028160
  192.3 72.5 %all-gather.9.cloned.1.call-done = f32[4,1,250880]{2,1,0:T(1,128)} async-done(((f32[1,1,250880]{2,1,0:T(1,128)}), f32[4,1,250880]{2,1,0:T(1,128)}) %all-gather.9.cloned.1.call-update) | async-done | bytes 4014096 | tf_op jit(solution)/shard_map/all_gather | solution.py:15
  264.9 5.5 %copy.29 = f32[4,1,250880]{2,0,1:T(4,128)} copy(f32[4,1,250880]{2,1,0:T(1,128)} %all-gather.9.cloned.1.call-done) | data formatting | bytes 8028160
  270.3 0.1 broadcast.33
  270.4 0.1 broadcast.33.clone
  270.5 22.3 %while.14 = (s32[]{:T(128)}, f32[250880]{0:T(1024)S(1)}, f32[250880]{0:T(1024)S(1)}, f32[1]{0:T(128)}, s32[]{:T(128)}, /*index=5*/f32[4,250880]{1,0:T(4,128)}, f...) while((s32[]{:T(128)}, f32[250880]{0:T(1024)S(1)}, ...), condition=%wide.region_2.3_spmd, body=%wide.region_1.2_spmd.sunk | while | flops 1254409 | bytes 10035413 | solution.py:23
  270.5 0.6 constant_dynamic-slice_fusion.6
  271.6 4.7 constant_dynamic-slice_fusion.5
  276.3 0.8 multiply_add_fusion.4
  277.7 0.6 constant_dynamic-slice_fusion.6
  278.9 5.1 %constant_dynamic-slice_fusion.5 = (f32[1,250880]{1,0:T(1,128)S(1)}, f32[1,250880]{1,0:T(1,128)S(1)}) fusion(f32[4,250880]{1,0:T(4,128)} %get-tuple-element.175, s32[]{:T(128)S(6)} %select_n.8, f32[4,250880]{1,0:T(4,128)} %get-tuple-element.173), kind=kLoop, calls=%fused_computation.2.clone.1 | loop fusion | bytes 4014084 | tf_op jit(solution)/shard_map/while/body/jit(dynamic_index_in_dim)/dynamic_slice | solution.py:20
  284.0 0.8 multiply_add_fusion.4
  285.4 0.6 constant_dynamic-slice_fusion.6
  286.6 4.5 constant_dynamic-slice_fusion.5
  291.1 0.8 multiply_add_fusion.4
  295.9 3.5 add_add_fusion.1
  299.4 1.8 stack.9
  301.2 0.4 copy.18
  301.5 0.0 copy-start
  301.5 3.0 stack.10
  304.5 2.7 copy.19
  307.2 0.0 copy-done
  307.2 3.7 fusion
  311.0 0.7 fusion.2
  311.7 2.4 copy.21
  314.0 0.5 copy.25
  314.5 131.3 %all-gather.7.cloned.1.call-done = bf16[2240,2240]{1,0:T(8,128)(2,1)} async-done(((bf16[560,2240]{1,0:T(8,128)(2,1)}), bf16[2240,2240]{1,0:T(8,128)(2,1)}) %all-gather.7.cloned.1.call-update) | async-done | bytes 10035216 | tf_op jit(solution)/shard_map/all_gather | solution.py:105
  445.9 13.4 %convolution_convert_fusion = bf16[512,2240]{0,1:T(8,128)(2,1)} fusion(bf16[512,2240]{0,1:T(8,128)(2,1)S(1)} %bitcast.74, bf16[2240,2240]{1,0:T(8,128)(2,1)} %all-gather.7.cloned.1.call-done), kind=kOutput, calls=%fused_computation.10 | convolution fusion | flops 5139169280 | bytes 14622720 | tf_op jit(solution)/shard_map/dot_general | solution.py:103
  459.3 4.8 %reshape.42 = bf16[2,2,128,2240]{2,1,0,3:T(2,128)(2,1)S(1)} reshape(bf16[512,2240]{0,1:T(8,128)(2,1)} %convolution_convert_fusion) | data formatting | bytes 4587520 | tf_op jit(solution)/shard_map/reshape | solution.py:108
  464.2 1.7 copy.22
  (6 shorter events, 0.0 us)
Async XLA Ops:
  6.5 96.9 %all-reduce.3.cloned.1.call-start = ((), (), s32[]{:S(2)}) async-start(), calls=%async_computation | async-start | bytes 4014080 | tf_op jit(solution)/shard_map/psum | solution.py:87
  46.5 5.6 %copy-start.3 = (s32[2]{0:T(128)S(1)}, s32[2]{0:T(128)}, u32[]{:S(2)}) copy-start(s32[2]{0:T(128)} %param.13) | copy-start | bytes 28
  46.5 5.7 %copy-start.5 = (u32[32]{0:T(128)S(1)}, u32[32]{0:T(128)}, u32[]{:S(2)}) copy-start(u32[32]{0:T(128)} %constant.52) | copy-start | bytes 388
  46.5 9.4 %copy-start.4 = (s32[2]{0:T(128)S(1)}, s32[2]{0:T(128)}, u32[]{:S(2)}) copy-start(s32[2]{0:T(128)} %param.12) | copy-start | bytes 28
  52.0 134.8 %all-gather.11.cloned.1.call-start = ((), (), s32[]{:S(2)}) async-start(), calls=%async_computation.3 | async-start | bytes 5017600 | tf_op jit(solution)/shard_map/all_gather | solution.py:15
  111.4 7.7 %copy-start.1 = (bf16[2,2,128,2240]{2,3,1,0:T(8,128)(2,1)S(1)}, bf16[2,2,128,2240]{2,3,1,0:T(8,128)(2,1)}, u32[]{:S(2)}) copy-start(bf16[2,2,128,2240]{2,3,1,0:T(8,128)(2,1)} %param.9) | copy-start | bytes 6881284
  111.4 153.4 %all-gather.9.cloned.1.call-start = ((), (), s32[]{:S(2)}) async-start(), calls=%async_computation.2 | async-start | bytes 5017600 | tf_op jit(solution)/shard_map/all_gather | solution.py:15
  112.1 333.7 %all-gather.7.cloned.1.call-start = ((), (), s32[]{:S(2)}) async-start(), calls=%async_computation.1 | async-start | bytes 12902400 | tf_op jit(solution)/shard_map/all_gather | solution.py:105
  129.3 2.8 copy-start.2
  301.5 5.7 %copy-start = (bf16[2,256,20,112]{1,3,2,0:T(8,128)(2,1)S(1)}, bf16[2,256,20,112]{1,3,2,0:T(8,128)(2,1)}, u32[]{:S(2)}) copy-start(bf16[2,256,20,112]{1,3,2,0:T(8,128)(2,1)} %reshape.40) | copy-start | bytes 6881284
Sparse Core Ops, SparseCore 0:
  52.2 51.2 all-reduce.2
  111.5 75.2 all-gather.10
  188.5 76.2 all-gather.8
  266.3 179.4 all-gather.6
where the time goes:
time: 478 us; the launch traced here: 472 us
  waiting for transfers between devices  307 us (64%)
  local copies, waits for them, and re-layouts  98.3 us (21%)
  matrix products  21 us (4%)
  between operations  18.3 us (4%)
  other arithmetic  17.9 us (4%)
  blocking collectives  6.39 us (1%)
    all_gather x1, waiting for transfers between devices, local(): lax.all_gather(out_weight, 'frm', axis=0, tiled=True)  131 us
    all_gather x2, waiting for transfers between devices, entering(): gathered = jax.tree.map(lambda a: lax.all_gather(a, axis), part)  127 us
    psum x1, waiting for transfers between devices, local(): summed = lax.psum(partial_value, 'row')  46.9 us
    unnamed x18, local copies, waits for them, and re-layouts  24.6 us
    dynamic_slice x6, local copies, waits for them, and re-layouts, one(): lax.dynamic_index_in_dim(a, step, 0, False)  16 us
    dot_general x1, matrix products, local(): jnp.dot(normed, lax.all_gather(out_weight, 'frm', axis=0, tiled=True), pr...  13.4 us
    max x1, local copies, waits for them, and re-layouts, local(): key_pos = jax.nn.relu(keys).reshape(frames, tokens, HEADS, HD)  10.3 us
    max x1, local copies, waits for them, and re-layouts, local(): jax.nn.relu(queries).reshape(frames, tokens, HEADS, HD).astype(jnp.float32)  10.1 us
  transfers between devices with their start and end apart: 4, of which 4 were waited for; matrix products, arithmetic and copies ran while one was open for 13% of the time, Pallas kernels for 0%

commit v1 on v0

--- a/solution.py
+++ b/solution.py
@@ -1,7 +1,11 @@
+import functools
+
 import jax
 import jax.numpy as jnp
 from jax import lax
 from jax.sharding import PartitionSpec as P
+from jax.experimental import pallas as pl
+from jax.experimental.pallas import tpu as pltpu
 
 HEADS = 20
 HD = 112
@@ -108,6 +112,381 @@
     return projected.astype(jnp.bfloat16).reshape(frames, lat_rows, lat_cols, model_width)
 
 
+MESH = pl.DeviceIdType.MESH
+F32 = jnp.float32
+BF16 = jnp.bfloat16
+
+
+def round_up(size, unit):
+    return (size + unit - 1) // unit * unit
+
+
+def fused(
+    planes, grp_axis, frm_axis, row_axis,
+    q_hbm, k_hbm, v_hbm, w_hbm, gain_ref, flag_ref, block_ref, out_ref,
+    qv, kv, vv, wv, part, sent, mate_in, x_out, x_in, own, chain_in, chain_out, reads, normed,
+    load_sem, zs_up, zs_dn, zr, xs, xr, ys, yr, ds, dr, ms, mr,
+    ps, pr, qs, qr, cs, cr, gs, gr,
+):
+    g, z, r = lax.axis_index(grp_axis), lax.axis_index(frm_axis), lax.axis_index(row_axis)
+    x, c = r // 2, r % 2
+    mate = (g, z, 2 * x + 1 - c)
+    xn = (g, z, 2 * (1 - x) + c)
+    yn = (1 - g, z, r)
+    up = (g, z + 1, r)
+    dn = (g, z - 1, r)
+    p_own, p_x, p_y, p_d = 2 * x + g, 2 * (1 - x) + g, 2 * x + 1 - g, 2 * (1 - x) + 1 - g
+    frames, tokens, width = qv.shape
+    groups, per = part.shape[0], part.shape[1]
+    rows, cols = wv.shape[1] // 4, wv.shape[2] // 2
+    depth = normed.shape[2]
+
+    def cut(p, core):
+        return (
+            pl.ds(pl.multiple_of(p * rows, 16), rows),
+            pl.ds(pl.multiple_of(core * cols, 128), cols),
+        )
+
+    def piece(s, p, core):
+        return wv.at[(s,) + cut(p, core)]
+
+    def remote(src, dst, send, recv, to):
+        return pltpu.make_async_remote_copy(
+            src_ref=src, dst_ref=dst, send_sem=send, recv_sem=recv,
+            device_id=to, device_id_type=MESH,
+        )
+
+    barrier = pltpu.get_barrier_semaphore()
+    for other in (mate, xn, yn):
+        pl.semaphore_signal(barrier, inc=1, device_id=other, device_id_type=MESH)
+
+    @pl.when(z > 0)
+    def _():
+        pl.semaphore_signal(barrier, inc=1, device_id=dn, device_id_type=MESH)
+
+    @pl.when(z < planes - 1)
+    def _():
+        pl.semaphore_signal(barrier, inc=1, device_id=up, device_id_type=MESH)
+
+    loads = [
+        pltpu.make_async_copy(k_hbm, kv, load_sem.at[0]),
+        pltpu.make_async_copy(v_hbm, vv, load_sem.at[1]),
+        pltpu.make_async_copy(q_hbm, qv, load_sem.at[2]),
+        pltpu.make_async_copy(w_hbm, wv.at[z], load_sem.at[3]),
+    ]
+    for load in loads:
+        load.start()
+    inner = (z > 0) & (z < planes - 1)
+
+    @pl.when(inner)
+    def _():
+        pl.semaphore_wait(barrier, 5)
+
+    @pl.when(jnp.logical_not(inner))
+    def _():
+        pl.semaphore_wait(barrier, 4)
+
+    def first_up():
+        return remote(w_hbm.at[cut(p_own, c)], piece(z, p_own, c), zs_up.at[z], zr.at[z], up)
+
+    def first_dn():
+        return remote(w_hbm.at[cut(p_own, c)], piece(z, p_own, c), zs_dn.at[z], zr.at[z], dn)
+
+    @pl.when(z < planes - 1)
+    def _():
+        first_up().start()
+
+    @pl.when(z > 0)
+    def _():
+        first_dn().start()
+
+    def shard_at(i):
+        near = jnp.minimum(z, planes - 1 - z)
+        s = jnp.where(i - 1 >= near, i, i - 1)
+        return jnp.where(z * 2 < planes, s, planes - 1 - s)
+
+    def z_up(s):
+        return remote(piece(s, p_own, c), piece(s, p_own, c), zs_up.at[s], zr.at[s], up)
+
+    def z_dn(s):
+        return remote(piece(s, p_own, c), piece(s, p_own, c), zs_dn.at[s], zr.at[s], dn)
+
+    def x_copy(s):
+        return remote(piece(s, p_own, c), piece(s, p_own, c), xs.at[s], xr.at[s], xn)
+
+    def y_copy(s):
+        return remote(piece(s, p_own, c), piece(s, p_own, c), ys.at[s], yr.at[s], yn)
+
+    def d_copy(s):
+        return remote(piece(s, p_x, c), piece(s, p_x, c), ds.at[s], dr.at[s], yn)
+
+    def m_copy(s, kind):
+        p = (p_own, p_x, p_y, p_d)[kind]
+        return remote(piece(s, p, c), piece(s, p, c), ms.at[s, kind], mr.at[s, kind], mate)
+
+    def landed(s, p, core, sem):
+        pltpu.make_async_copy(piece(s, p, core), piece(s, p, core), sem).wait()
+
+    def stage_z(i):
+        s = shard_at(i)
+        landed(s, p_own, c, zr.at[s])
+
+        @pl.when((s < z) & (z < planes - 1))
+        def _():
+            z_up(s).start()
+
+        @pl.when((s > z) & (z > 0))
+        def _():
+            z_dn(s).start()
+
+        x_copy(s).start()
+        y_copy(s).start()
+        m_copy(s, 0).start()
+
+    def stage_xy(i):
+        s = shard_at(i)
+        landed(s, p_x, c, xr.at[s])
+        d_copy(s).start()
+        m_copy(s, 1).start()
+        landed(s, p_y, c, yr.at[s])
+        m_copy(s, 2).start()
+
+    def stage_d(i):
+        s = shard_at(i)
+        landed(s, p_d, c, dr.at[s])
+        m_copy(s, 3).start()
+
+    def stage_m(i):
+        s = shard_at(i)
+        for kind, p in enumerate((p_own, p_x, p_y, p_d)):
+            landed(s, p, 1 - c, mr.at[s, kind])
+
+    def finish(i):
+        s = shard_at(i)
+
+        @pl.when((s < z) & (z < planes - 1))
+        def _():
+            z_up(s).wait_send()
+
+        @pl.when((s > z) & (z > 0))
+        def _():
+            z_dn(s).wait_send()
+
+        x_copy(s).wait_send()
+        y_copy(s).wait_send()
+        d_copy(s).wait_send()
+        for kind in range(4):
+            m_copy(s, kind).wait_send()
+
+    loads[0].wait()
+    loads[1].wait()
+
+    def state_step(f, carry):
+        for h in range(groups * per):
+            lanes = slice(h * HD, (h + 1) * HD)
+            key = jnp.maximum(kv[f, :, lanes], jnp.zeros((), BF16))
+            state = lax.dot_general(
+                key, vv[f, :, lanes], (((0,), (0,)), ((), ())), preferred_element_type=F32
+            )
+            part[h // per, h % per, f] = state
+            sent[h // per, h % per, f] = state.astype(BF16)
+        return carry
+
+    lax.fori_loop(0, frames, state_step, 0)
+
+    mate_sums = [
+        remote(sent.at[2 * chip + 1 - c], mate_in.at[chip], ps.at[chip], pr.at[chip], mate)
+        for chip in range(groups // 2)
+    ]
+    for copy in mate_sums:
+        copy.start()
+    for copy in mate_sums:
+        copy.wait_recv()
+    x_out[...] = (part[2 * (1 - x) + c] + mate_in[1 - x].astype(F32)).astype(BF16)
+    x_sum = remote(x_out, x_in, qs, qr, xn)
+    x_sum.start()
+    own[...] = part[r] + mate_in[x].astype(F32)
+    stage_z(1)
+    x_sum.wait_recv()
+
+    @pl.when(z == 0)
+    def _():
+        chain_in[:, :, :HD, :] = jnp.zeros((per, 2, HD, HD), BF16)
+        chain_in[:, :, HD:, :] = jnp.full((per, 2, chain_in.shape[2] - HD, HD), -1.0, BF16)
+
+    def chain_copy(h):
+        return remote(chain_out.at[h], chain_in.at[h], cs.at[h], cr.at[h], up)
+
+    for h in range(per):
+
+        @pl.when(z > 0)
+        def _():
+            pltpu.make_async_copy(chain_in.at[h], chain_in.at[h], cr.at[h]).wait()
+
+        closed = chain_in[h, 0, :HD, :].astype(F32)
+        opened = chain_in[h, 1, :HD, :].astype(F32)
+        latest = chain_in[h, 0, HD:, :].astype(F32)[:1]
+        for f in range(frames):
+            summed = own[h, f] + x_in[h, f].astype(F32)
+            flag = flag_ref[f].astype(F32)
+            block = block_ref[f].astype(F32)
+            advance = jnp.where(latest < block, 1.0, 0.0)
+            select = jnp.maximum(advance, flag)
+            reads[r, h, f] = (closed + select * opened + summed).astype(BF16)
+            closed = closed + advance * opened
+            opened = flag * summed + (1.0 - advance) * opened
+            latest = jnp.maximum(latest, block)
+
+        @pl.when(z < planes - 1)
+        def _():
+            chain_out[h, 0, :HD, :] = closed.astype(BF16)
+            chain_out[h, 1, :HD, :] = opened.astype(BF16)
+            chain_out[h, 0, HD:, :] = jnp.broadcast_to(
+                latest, (chain_in.shape[2] - HD, HD)
+            ).astype(BF16)
+            chain_copy(h).start()
+
+    other_x = 2 * (1 - x) + c
+    read_mate = remote(reads.at[r], reads.at[r], gs.at[0], gr.at[0], mate)
+    read_x = remote(reads.at[r], reads.at[r], gs.at[1], gr.at[1], xn)
+    relay = remote(reads.at[other_x], reads.at[other_x], gs.at[2], gr.at[2], mate)
+    read_x.start()
+    read_mate.start()
+    stage_xy(1)
+    stage_z(2)
+
+    def got(group, sem):
+        pltpu.make_async_copy(reads.at[group], reads.at[group], sem).wait()
+
+    got(other_x, gr.at[1])
+    relay.start()
+    stage_d(1)
+    stage_xy(2)
+    stage_z(3) if planes > 3 else None
+    got(2 * x + 1 - c, gr.at[0])
+    got(2 * (1 - x) + 1 - c, gr.at[2])
+    loads[2].wait()
+
+    def read_step(f, carry):
+        for h in range(groups * per):
+            lanes = slice(h * HD, (h + 1) * HD)
+            query = jnp.maximum(qv[f, :, lanes], jnp.zeros((), BF16))
+            attended = jnp.dot(
+                query, reads[h // per, h % per, f], preferred_element_type=F32
+            )
+            mean = jnp.sum(attended * attended, axis=-1, keepdims=True) * (1.0 / HD)
+            value = attended * lax.rsqrt(mean + norm_eps) * gain_ref[h : h + 1, :]
+            at = h * HD % depth
+            normed[h * HD // depth, pl.ds(pl.multiple_of(f * tokens, tokens), tokens), at : at + HD] = (
+                value.astype(BF16)
+            )
+        return carry
+
+    lax.fori_loop(0, frames, read_step, 0)
+    for i in range(4, planes):
+        stage_z(i)
+    for i in range(3, planes):
+        stage_xy(i)
+    for i in range(2, planes):
+        stage_d(i)
+    for i in range(1, planes):
+        stage_m(i)
+    loads[3].wait()
+
+    def project(lanes):
+        total = jnp.dot(normed[0], wv[0, :depth, lanes], preferred_element_type=F32)
+        for s in range(1, planes):
+            total += jnp.dot(normed[s], wv[s, :depth, lanes], preferred_element_type=F32)
+        out_ref[:, lanes] = total.astype(BF16)
+
+    tile = 256
+
+    def project_step(n, carry):
+        project(pl.ds(pl.multiple_of(n * tile, tile), tile))
+        return carry
+
+    lax.fori_loop(0, width // tile, project_step, 0)
+    if width % tile:
+        project(slice(width // tile * tile, width))
+
+    @pl.when(z < planes - 1)
+    def _():
+        first_up().wait_send()
+        for h in range(per):
+            chain_copy(h).wait_send()
+
+    @pl.when(z > 0)
+    def _():
+        first_dn().wait_send()
+
+    for i in range(1, planes):
+        finish(i)
+    for copy in mate_sums:
+        copy.wait_send()
+    x_sum.wait_send()
+    read_mate.wait_send()
+    read_x.wait_send()
+    relay.wait_send()
+
+
+def local_fused(mesh_shape, queries, keys, values, flags, blocks, out_weight, norm_gain):
+    frames, lat_rows, lat_cols, width = queries.shape
+    tokens = lat_rows * lat_cols
+    planes, groups = mesh_shape["frm"], mesh_shape["row"]
+    per = HEADS // groups
+    depth = out_weight.shape[0]
+    rows, cols = round_up(depth, 64), round_up(width, 256)
+    weight = jnp.pad(out_weight, ((0, rows - depth), (0, cols - width)))
+    dma = pltpu.SemaphoreType.DMA
+    shape = (frames, tokens, width)
+    anywhere = pl.BlockSpec(memory_space=pl.ANY)
+    scalar = pl.BlockSpec(memory_space=pltpu.SMEM)
+    vector = pl.BlockSpec(memory_space=pltpu.VMEM)
+    per_group = (per, frames, HD, HD)
+    link = (per, 2, round_up(HD + 1, 16), HD)
+    out = pl.pallas_call(
+        functools.partial(fused, planes, "grp", "frm", "row"),
+        out_shape=jax.ShapeDtypeStruct((frames * tokens, width), BF16),
+        in_specs=[anywhere] * 4 + [vector, scalar, scalar],
+        out_specs=vector,
+        scratch_shapes=[
+            pltpu.VMEM(shape, BF16),
+            pltpu.VMEM(shape, BF16),
+            pltpu.VMEM(shape, BF16),
+            pltpu.VMEM((planes, rows, cols), BF16),
+            pltpu.VMEM((groups,) + per_group, F32),
+            pltpu.VMEM((groups,) + per_group, BF16),
+            pltpu.VMEM((groups // 2,) + per_group, BF16),
+            pltpu.VMEM(per_group, BF16),
+            pltpu.VMEM(per_group, BF16),
+            pltpu.VMEM(per_group, F32),
+            pltpu.VMEM(link, BF16),
+            pltpu.VMEM(link, BF16),
+            pltpu.VMEM((groups,) + per_group, BF16),
+            pltpu.VMEM((planes, frames * tokens, depth), BF16),
+            dma((4,)),
+        ]
+        + [dma((planes,))] * 9
+        + [dma((planes, 4))] * 2
+        + [dma((groups // 2,))] * 2
+        + [dma(()), dma(())]
+        + [dma((per,))] * 2
+        + [dma((3,))] * 2,
+        compiler_params=pltpu.CompilerParams(
+            collective_id=0, has_side_effects=True, vmem_limit_bytes=56 * 1024 * 1024
+        ),
+    )(
+        queries.reshape(shape), keys.reshape(shape), values.reshape(shape), weight,
+        norm_gain.reshape(HEADS, HD), flags, blocks,
+    )
+    return out.reshape(queries.shape)
+
+
+def fits(mesh):
+    grp, frm, row = mesh.shape["grp"], mesh.shape["frm"], mesh.shape["row"]
+    return grp == 2 and row == 4 and frm > 2 and HEADS % row == 0 and HEADS % frm == 0
+
+
 def solution(mesh):
     in_specs = (
         P(("grp", "frm"), "row", None, None),
@@ -119,4 +498,5 @@
         P(),
     )
     out_specs = P(("grp", "frm"), "row", None, None)
-    return jax.shard_map(local, mesh=mesh, in_specs=in_specs, out_specs=out_specs, check_vma=False)
+    body = functools.partial(local_fused, dict(mesh.shape)) if fits(mesh) else local
+    return jax.shard_map(body, mesh=mesh, in_specs=in_specs, out_specs=out_specs, check_vma=False)

time: 478 us -> 102 us (0.21); the launches traced: 472 us -> 101 us
  waiting for transfers between devices: 307 us -> 0 us
  Pallas kernels: 0 us -> 82.4 us
  local copies, waits for them, and re-layouts: 98.3 us -> 19 us
  matrix products: 21 us -> 0 us
  between operations: 18.3 us -> 0.01 us
  other arithmetic: 17.9 us -> 0 us
  blocking collectives: 6.39 us -> 0 us
    all_gather x3 -> x0, waiting for transfers between devices: 259 us -> none  [the longest x1 131 us: local(): lax.all_gather(out_weight, 'frm', axis=0, tiled=True)]
    pallas_call x0 -> x1, Pallas kernels: none -> 82.4 us  [local_fused(): pl.pallas_call(functools.partial(fused, planes, 'grp', 'frm', 'row'), out...]
    psum x1 -> x0, waiting for transfers between devices: 46.9 us -> none  [local(): summed = lax.psum(partial_value, 'row')]
    dot_general x3 -> x0, matrix products: 21 us -> none  [the longest x1 13.4 us: local(): jnp.dot(normed, lax.all_gather(out_weight, 'frm', axis=0, tiled=True), pr...]
    reshape x6 -> x2, local copies, waits for them, and re-layouts: 26.3 us -> 5.78 us  [the longest x1 4.25 us: local_fused(): return out.reshape(queries.shape)]
    max x2 -> x0, local copies, waits for them, and re-layouts: 20.4 us -> none  [the longest x1 10.3 us: local(): key_pos = jax.nn.relu(keys).reshape(frames, tokens, HEADS, HD)]
    dynamic_slice x6 -> x0, local copies, waits for them, and re-layouts: 16 us -> none  [one(): lax.dynamic_index_in_dim(a, step, 0, False)]
    unnamed x18 -> x7, local copies, waits for them, and re-layouts: 24.6 us -> 11.5 us
  transfers between devices with their start and end apart: 4 -> 0, of which waited for: 4 -> 0; matrix products, arithmetic and copies ran while one was open for 13% -> 0% of each run, Pallas kernels for 0% -> 0%
where the time goes in v1:
time: 102 us; the launch traced here: 101 us
  Pallas kernels  82.4 us (81%)
  local copies, waits for them, and re-layouts  19 us (19%)
    pallas_call x1, Pallas kernels, local_fused(): pl.pallas_call(functools.partial(fused, planes, 'grp', 'frm', 'row'), out...  82.4 us
    unnamed x7, local copies, waits for them, and re-layouts  11.5 us
    reshape x1, local copies, waits for them, and re-layouts, local_fused(): return out.reshape(queries.shape)  4.25 us

profile of v1, /device:TPU:25, one launch (start us, length us, event | category | flops | bytes accessed | tf_op | source)
XLA Modules:
  0.0 101.4 jit_solution(4755298147862823942)
XLA Ops:
  0.0 0.0 copy-start.1
  0.0 1.5 %reshape.18.gain_ref = f32[20,112]{1,0:T(8,128)} reshape(f32[2240]{0:T(1024)} %param.13) | data formatting | bytes 17920 | tf_op jit(solution)/shard_map/reshape | solution.py:480
  1.5 4.2 %copy.8 = bf16[2,2,128,2240]{3,2,1,0:T(8,128)(2,1)} copy(bf16[2,2,128,2240]{2,3,1,0:T(8,128)(2,1)} %param.7) | data formatting | bytes 4587520 | tf_op args[0]
  5.8 0.0 copy-done.1
  5.8 2.8 %copy.9 = bf16[2,2,128,2240]{3,2,1,0:T(8,128)(2,1)} copy(bf16[2,2,128,2240]{2,3,1,0:T(8,128)(2,1)S(1)} %copy-done.1) | data formatting | bytes 4587520 | tf_op args[1]
  8.6 0.0 copy-start
  8.6 4.5 %copy.10 = bf16[2,2,128,2240]{3,2,1,0:T(8,128)(2,1)} copy(bf16[2,2,128,2240]{2,3,1,0:T(8,128)(2,1)} %param.9) | data formatting | bytes 4587520 | tf_op args[2]
  13.1 0.0 copy-done
  13.1 1.7 %pad.4.w_hbm = bf16[576,2304]{1,0:T(8,128)(2,1)} pad(bf16[560,2240]{1,0:T(8,128)(2,1)S(1)} %copy-done, bf16[]{:T(256)} %constant.2.clone.1), padding=0_16x0_64 | pad | bytes 5163010 | tf_op jit(solution)/shard_map/jit(_pad)/pad | solution.py:439
  14.8 82.4 %shard_map.73 = bf16[512,2240]{1,0:T(8,128)(2,1)} custom-call(bf16[2,256,2240]{2,1,0:T(8,128)(2,1)} %bitcast.4, bf16[2,256,2240]{2,1,0:T(8,128)(2,1)} %bitcast.5, bf16[2,256,2240]{2,1,0:T(8,128)(2,1)} %bitcast.6, bf16[576,2304]{1,0:T(8,128)(2,1)} %pad.4.w_hbm, f32[20,112]{1,0:T(8,128)} %reshape.18.gain_ref, s32[2]{0:T(128)} %flag_ref.1, s32[2]{0:T(128)} %block_ref.1), custom_call_target="tpu_custom_call" | custom-call | tf_op jit(solution)/shard_map/pallas_call | solution.py:447
  97.1 4.3 %copy.11 = bf16[2,2,128,2240]{2,3,1,0:T(8,128)(2,1)} copy(bf16[2,2,128,2240]{3,2,1,0:T(8,128)(2,1)} %bitcast.7) | data formatting | bytes 4587520 | tf_op jit(solution)/shard_map/reshape | solution.py:482
Async XLA Ops:
  0.0 5.8 %copy-start.1 = (bf16[2,2,128,2240]{2,3,1,0:T(8,128)(2,1)S(1)}, bf16[2,2,128,2240]{2,3,1,0:T(8,128)(2,1)}, u32[]{:S(2)}) copy-start(bf16[2,2,128,2240]{2,3,1,0:T(8,128)(2,1)} %param.8) | copy-start | bytes 6881284
  8.6 4.5 %copy-start = (bf16[560,2240]{1,0:T(8,128)(2,1)S(1)}, bf16[560,2240]{1,0:T(8,128)(2,1)}, u32[]{:S(2)}) copy-start(bf16[560,2240]{1,0:T(8,128)(2,1)} %param.12) | copy-start | bytes 7526404

commit v2 on v1

--- a/solution.py
+++ b/solution.py
@@ -124,7 +124,7 @@
 def fused(
     planes, grp_axis, frm_axis, row_axis,
     q_hbm, k_hbm, v_hbm, w_hbm, gain_ref, flag_ref, block_ref, out_ref,
-    qv, kv, vv, wv, part, sent, mate_in, x_out, x_in, own, chain_in, chain_out, reads, normed,
+    qv, kv, vv, wv, part, sent, mate_in, x_out, x_in, own, chain_in, chain_out, reads, normed, gains,
     load_sem, zs_up, zs_dn, zr, xs, xr, ys, yr, ds, dr, ms, mr,
     ps, pr, qs, qr, cs, cr, gs, gr,
 ):
@@ -136,10 +136,11 @@
     up = (g, z + 1, r)
     dn = (g, z - 1, r)
     p_own, p_x, p_y, p_d = 2 * x + g, 2 * (1 - x) + g, 2 * x + 1 - g, 2 * (1 - x) + 1 - g
-    frames, tokens, width = qv.shape
+    frames, lat_rows, width, lat_cols = qv.shape
+    tokens = lat_rows * lat_cols
     groups, per = part.shape[0], part.shape[1]
     rows, cols = wv.shape[1] // 4, wv.shape[2] // 2
-    depth = normed.shape[2]
+    depth = normed.shape[1]
 
     def cut(p, core):
         return (
@@ -281,12 +282,15 @@
     loads[0].wait()
     loads[1].wait()
 
+    def head_of(ref, f, h):
+        span = slice(h * HD, (h + 1) * HD)
+        return jnp.concatenate([ref[f, row, span, :] for row in range(lat_rows)], axis=1)
+
     def state_step(f, carry):
         for h in range(groups * per):
-            lanes = slice(h * HD, (h + 1) * HD)
-            key = jnp.maximum(kv[f, :, lanes], jnp.zeros((), BF16))
+            key = jnp.maximum(head_of(kv, f, h), jnp.zeros((), BF16))
             state = lax.dot_general(
-                key, vv[f, :, lanes], (((0,), (0,)), ((), ())), preferred_element_type=F32
+                head_of(vv, f, h), key, (((1,), (1,)), ((), ())), preferred_element_type=F32
             )
             part[h // per, h % per, f] = state
             sent[h // per, h % per, f] = state.astype(BF16)
@@ -300,6 +304,12 @@
     ]
     for copy in mate_sums:
         copy.start()
+    diagonal = (
+        lax.broadcasted_iota(jnp.int32, (HD, HD), 0) == lax.broadcasted_iota(jnp.int32, (HD, HD), 1)
+    ).astype(F32)
+    for h in range(groups * per):
+        span = slice(h * HD, (h + 1) * HD)
+        gains[span, :] = jnp.sum(diagonal * gain_ref[:, span], axis=1, keepdims=True)
     for copy in mate_sums:
         copy.wait_recv()
     x_out[...] = (part[2 * (1 - x) + c] + mate_in[1 - x].astype(F32)).astype(BF16)
@@ -316,6 +326,14 @@
 
     def chain_copy(h):
         return remote(chain_out.at[h], chain_in.at[h], cs.at[h], cr.at[h], up)
+
+    upper = z * 2 >= planes
+
+    def early():
+        stage_xy(1)
+        stage_z(2)
+
+    pl.when(upper)(early)
 
     for h in range(per):
 
@@ -352,8 +370,7 @@
     relay = remote(reads.at[other_x], reads.at[other_x], gs.at[2], gr.at[2], mate)
     read_x.start()
     read_mate.start()
-    stage_xy(1)
-    stage_z(2)
+    pl.when(jnp.logical_not(upper))(early)
 
     def got(group, sem):
         pltpu.make_async_copy(reads.at[group], reads.at[group], sem).wait()
@@ -369,15 +386,14 @@
 
     def read_step(f, carry):
         for h in range(groups * per):
-            lanes = slice(h * HD, (h + 1) * HD)
-            query = jnp.maximum(qv[f, :, lanes], jnp.zeros((), BF16))
+            query = jnp.maximum(head_of(qv, f, h), jnp.zeros((), BF16))
             attended = jnp.dot(
-                query, reads[h // per, h % per, f], preferred_element_type=F32
+                reads[h // per, h % per, f], query, preferred_element_type=F32
             )
-            mean = jnp.sum(attended * attended, axis=-1, keepdims=True) * (1.0 / HD)
-            value = attended * lax.rsqrt(mean + norm_eps) * gain_ref[h : h + 1, :]
+            mean = jnp.sum(attended * attended, axis=0, keepdims=True) * (1.0 / HD)
+            value = attended * lax.rsqrt(mean + norm_eps) * gains[h * HD : (h + 1) * HD, :]
             at = h * HD % depth
-            normed[h * HD // depth, pl.ds(pl.multiple_of(f * tokens, tokens), tokens), at : at + HD] = (
+            normed[h * HD // depth, at : at + HD, pl.ds(pl.multiple_of(f * tokens, tokens), tokens)] = (
                 value.astype(BF16)
             )
         return carry
@@ -393,11 +409,19 @@
         stage_m(i)
     loads[3].wait()
 
+    def product(s, lanes):
+        return lax.dot_general(
+            wv[s, :depth, lanes], normed[s], (((0,), (0,)), ((), ())), preferred_element_type=F32
+        )
+
     def project(lanes):
-        total = jnp.dot(normed[0], wv[0, :depth, lanes], preferred_element_type=F32)
+        total = product(0, lanes)
         for s in range(1, planes):
-            total += jnp.dot(normed[s], wv[s, :depth, lanes], preferred_element_type=F32)
-        out_ref[:, lanes] = total.astype(BF16)
+            total += product(s, lanes)
+        for f in range(frames):
+            for row in range(lat_rows):
+                at = (f * lat_rows + row) * lat_cols
+                out_ref[f, row, lanes, :] = total[:, at : at + lat_cols].astype(BF16)
 
     tile = 256
 
@@ -431,14 +455,13 @@
 
 def local_fused(mesh_shape, queries, keys, values, flags, blocks, out_weight, norm_gain):
     frames, lat_rows, lat_cols, width = queries.shape
-    tokens = lat_rows * lat_cols
     planes, groups = mesh_shape["frm"], mesh_shape["row"]
     per = HEADS // groups
     depth = out_weight.shape[0]
     rows, cols = round_up(depth, 64), round_up(width, 256)
     weight = jnp.pad(out_weight, ((0, rows - depth), (0, cols - width)))
     dma = pltpu.SemaphoreType.DMA
-    shape = (frames, tokens, width)
+    shape = (frames, lat_rows, width, lat_cols)
     anywhere = pl.BlockSpec(memory_space=pl.ANY)
     scalar = pl.BlockSpec(memory_space=pltpu.SMEM)
     vector = pl.BlockSpec(memory_space=pltpu.VMEM)
@@ -446,7 +469,7 @@
     link = (per, 2, round_up(HD + 1, 16), HD)
     out = pl.pallas_call(
         functools.partial(fused, planes, "grp", "frm", "row"),
-        out_shape=jax.ShapeDtypeStruct((frames * tokens, width), BF16),
+        out_shape=jax.ShapeDtypeStruct(shape, BF16),
         in_specs=[anywhere] * 4 + [vector, scalar, scalar],
         out_specs=vector,
         scratch_shapes=[
@@ -463,7 +486,8 @@
             pltpu.VMEM(link, BF16),
             pltpu.VMEM(link, BF16),
             pltpu.VMEM((groups,) + per_group, BF16),
-            pltpu.VMEM((planes, frames * tokens, depth), BF16),
+            pltpu.VMEM((planes, depth, frames * lat_rows * lat_cols), BF16),
+            pltpu.VMEM((width, 1), F32),
             dma((4,)),
         ]
         + [dma((planes,))] * 9
@@ -476,10 +500,10 @@
             collective_id=0, has_side_effects=True, vmem_limit_bytes=56 * 1024 * 1024
         ),
     )(
-        queries.reshape(shape), keys.reshape(shape), values.reshape(shape), weight,
-        norm_gain.reshape(HEADS, HD), flags, blocks,
-    )
-    return out.reshape(queries.shape)
+        *(jnp.swapaxes(a, 2, 3) for a in (queries, keys, values)), weight,
+        norm_gain.reshape(1, width), flags, blocks,
+    )
+    return jnp.swapaxes(out, 2, 3)
 
 
 def fits(mesh):

time: 102 us -> 87.6 us (0.86)
  local copies, waits for them, and re-layouts: 19 us -> 7.93 us
  Pallas kernels: 82.4 us -> 79.4 us
    unnamed x7 -> x1, local copies, waits for them, and re-layouts: 11.5 us -> 3.18 us
    reshape x2 -> x1, local copies, waits for them, and re-layouts: 5.78 us -> 1.31 us  [local_fused(): norm_gain.reshape(1, width)]
    pallas_call x1, Pallas kernels: 82.4 us -> 79.4 us  [local_fused(): pl.pallas_call(functools.partial(fused, planes, 'grp', 'frm', 'row'), out...]
    pad x1, local copies, waits for them, and re-layouts: 1.7 us -> 3.44 us  [local_fused(): weight = jnp.pad(out_weight, ((0, rows - depth), (0, cols - width)))]
where the time goes in v2:
time: 87.6 us; the launch traced here: 87.3 us
  Pallas kernels  79.4 us (91%)
  local copies, waits for them, and re-layouts  7.93 us (9%)
    pallas_call x1, Pallas kernels, local_fused(): pl.pallas_call(functools.partial(fused, planes, 'grp', 'frm', 'row'), out...  79.4 us
    pad x1, local copies, waits for them, and re-layouts, local_fused(): weight = jnp.pad(out_weight, ((0, rows - depth), (0, cols - width)))  3.44 us
    unnamed x1, local copies, waits for them, and re-layouts  3.18 us

profile of v2, /device:TPU:25, one launch (start us, length us, event | category | flops | bytes accessed | tf_op | source)
XLA Modules:
  0.0 87.3 jit_solution(6380098513123648243)
XLA Ops:
  0.0 1.3 %reshape.3.gain_ref = f32[1,2240]{1,0:T(1,128)} reshape(f32[2240]{0:T(1024)} %param.13) | data formatting | bytes 17920 | tf_op jit(solution)/shard_map/reshape | solution.py:504
  1.3 3.4 %pad.4.w_hbm = bf16[576,2304]{1,0:T(8,128)(2,1)} pad(bf16[560,2240]{1,0:T(8,128)(2,1)} %param.12, bf16[]{:T(256)} %constant.2.clone.1), padding=0_16x0_64 | pad | bytes 5163010 | tf_op jit(solution)/shard_map/jit(_pad)/pad | solution.py:462
  4.7 79.4 %shard_map.73 = bf16[2,2,2240,128]{3,2,1,0:T(8,128)(2,1)} custom-call(bf16[2,2,2240,128]{3,2,1,0:T(8,128)(2,1)} %bitcast.5, bf16[2,2,2240,128]{3,2,1,0:T(8,128)(2,1)} %bitcast.6, bf16[2,2,2240,128]{3,2,1,0:T(8,128)(2,1)} %bitcast.7, bf16[576,2304]{1,0:T(8,128)(2,1)} %pad.4.w_hbm, f32[1,2240]{1,0:T(1,128)} %reshape.3.gain_ref, s32[2]{0:T(128)} %flag_ref.1, ...), custom_call_target="tpu_custom_call" | custom-call | tf_op jit(solution)/shard_map/pallas_call | solution.py:470
  84.2 3.2 %copy.9 = bf16[2,2,128,2240]{2,3,1,0:T(8,128)(2,1)} copy(bf16[2,2,128,2240]{2,3,1,0:T(8,128)(2,1)} %bitcast.4) | data formatting | bytes 4587520

commit v3 on v2

--- a/solution.py
+++ b/solution.py
@@ -12,6 +12,7 @@
 
 
 norm_eps = 1e-06
+CHUNKS = 3
 
 
 def entering(part, axis, combine, identity):
@@ -124,7 +125,7 @@
 def fused(
     planes, grp_axis, frm_axis, row_axis,
     q_hbm, k_hbm, v_hbm, w_hbm, gain_ref, flag_ref, block_ref, out_ref,
-    qv, kv, vv, wv, part, sent, mate_in, x_out, x_in, own, chain_in, chain_out, reads, normed, gains,
+    qv, kv, vv, wv, part, sent, mate_in, x_out, x_in, own, chain_in, chain_out, reads, normed, gains, acc,
     load_sem, zs_up, zs_dn, zr, xs, xr, ys, yr, ds, dr, ms, mr,
     ps, pr, qs, qr, cs, cr, gs, gr,
 ):
@@ -142,14 +143,16 @@
     rows, cols = wv.shape[1] // 4, wv.shape[2] // 2
     depth = normed.shape[1]
 
-    def cut(p, core):
+    chunk = rows // CHUNKS
+
+    def cut(p, core, j):
         return (
-            pl.ds(pl.multiple_of(p * rows, 16), rows),
+            pl.ds(pl.multiple_of(p * rows + j * chunk, 16), chunk),
             pl.ds(pl.multiple_of(core * cols, 128), cols),
         )
 
-    def piece(s, p, core):
-        return wv.at[(s,) + cut(p, core)]
+    def piece(s, p, core, j):
+        return wv.at[(s,) + cut(p, core, j)]
 
     def remote(src, dst, send, recv, to):
         return pltpu.make_async_remote_copy(
@@ -187,97 +190,130 @@
     def _():
         pl.semaphore_wait(barrier, 4)
 
-    def first_up():
-        return remote(w_hbm.at[cut(p_own, c)], piece(z, p_own, c), zs_up.at[z], zr.at[z], up)
-
-    def first_dn():
-        return remote(w_hbm.at[cut(p_own, c)], piece(z, p_own, c), zs_dn.at[z], zr.at[z], dn)
-
-    @pl.when(z < planes - 1)
-    def _():
-        first_up().start()
-
-    @pl.when(z > 0)
-    def _():
-        first_dn().start()
+    along = [(p_own, j) for j in range(CHUNKS)] + [(p_d, 0)]
+
+    def first_up(n):
+        p, j = along[n]
+        return remote(w_hbm.at[cut(p, c, j)], piece(z, p, c, j), zs_up.at[z, n], zr.at[z, n], up)
+
+    def first_dn(n):
+        p, j = along[n]
+        return remote(w_hbm.at[cut(p, c, j)], piece(z, p, c, j), zs_dn.at[z, n], zr.at[z, n], dn)
+
+    for n in range(CHUNKS + 1):
+
+        @pl.when(z < planes - 1)
+        def _():
+            first_up(n).start()
+
+        @pl.when(z > 0)
+        def _():
+            first_dn(n).start()
 
     def shard_at(i):
         near = jnp.minimum(z, planes - 1 - z)
         s = jnp.where(i - 1 >= near, i, i - 1)
         return jnp.where(z * 2 < planes, s, planes - 1 - s)
 
-    def z_up(s):
-        return remote(piece(s, p_own, c), piece(s, p_own, c), zs_up.at[s], zr.at[s], up)
-
-    def z_dn(s):
-        return remote(piece(s, p_own, c), piece(s, p_own, c), zs_dn.at[s], zr.at[s], dn)
-
-    def x_copy(s):
-        return remote(piece(s, p_own, c), piece(s, p_own, c), xs.at[s], xr.at[s], xn)
-
-    def y_copy(s):
-        return remote(piece(s, p_own, c), piece(s, p_own, c), ys.at[s], yr.at[s], yn)
-
-    def d_copy(s):
-        return remote(piece(s, p_x, c), piece(s, p_x, c), ds.at[s], dr.at[s], yn)
-
-    def m_copy(s, kind):
+    def z_up(s, n):
+        p, j = along[n]
+        return remote(piece(s, p, c, j), piece(s, p, c, j), zs_up.at[s, n], zr.at[s, n], up)
+
+    def z_dn(s, n):
+        p, j = along[n]
+        return remote(piece(s, p, c, j), piece(s, p, c, j), zs_dn.at[s, n], zr.at[s, n], dn)
+
+    def x_copy(s, j):
+        return remote(piece(s, p_own, c, j), piece(s, p_own, c, j), xs.at[s, j], xr.at[s, j], xn)
+
+    def y_copy(s, j):
+        return remote(piece(s, p_own, c, j), piece(s, p_own, c, j), ys.at[s, j], yr.at[s, j], yn)
+
+    def d_copy(s, j):
+        return remote(piece(s, p_x, c, j), piece(s, p_x, c, j), ds.at[s, j], dr.at[s, j], yn)
+
+    def m_copy(s, kind, j):
         p = (p_own, p_x, p_y, p_d)[kind]
-        return remote(piece(s, p, c), piece(s, p, c), ms.at[s, kind], mr.at[s, kind], mate)
-
-    def landed(s, p, core, sem):
-        pltpu.make_async_copy(piece(s, p, core), piece(s, p, core), sem).wait()
-
-    def stage_z(i):
+        at = kind * CHUNKS + j
+        return remote(piece(s, p, c, j), piece(s, p, c, j), ms.at[s, at], mr.at[s, at], mate)
+
+    def landed(s, p, core, j, sem):
+        pltpu.make_async_copy(piece(s, p, core, j), piece(s, p, core, j), sem).wait()
+
+    def stage_z(i, n):
         s = shard_at(i)
-        landed(s, p_own, c, zr.at[s])
+        p, j = along[n]
+        landed(s, p, c, j, zr.at[s, n])
 
         @pl.when((s < z) & (z < planes - 1))
         def _():
-            z_up(s).start()
+            z_up(s, n).start()
 
         @pl.when((s > z) & (z > 0))
         def _():
-            z_dn(s).start()
-
-        x_copy(s).start()
-        y_copy(s).start()
-        m_copy(s, 0).start()
-
-    def stage_xy(i):
+            z_dn(s, n).start()
+
+        if n < CHUNKS:
+            y_copy(s, j).start()
+            x_copy(s, j).start()
+            m_copy(s, 0, j).start()
+        else:
+            m_copy(s, 3, j).start()
+
+    def stage_xy(i, j):
         s = shard_at(i)
-        landed(s, p_x, c, xr.at[s])
-        d_copy(s).start()
-        m_copy(s, 1).start()
-        landed(s, p_y, c, yr.at[s])
-        m_copy(s, 2).start()
-
-    def stage_d(i):
-        s = shard_at(i)
-        landed(s, p_d, c, dr.at[s])
-        m_copy(s, 3).start()
+        landed(s, p_x, c, j, xr.at[s, j])
+        if j > 0:
+            d_copy(s, j).start()
+        m_copy(s, 1, j).start()
+        landed(s, p_y, c, j, yr.at[s, j])
+        m_copy(s, 2, j).start()
+
+    def stage_d(i, j):
+        if j > 0:
+            s = shard_at(i)
+            landed(s, p_d, c, j, dr.at[s, j])
+            m_copy(s, 3, j).start()
 
     def stage_m(i):
         s = shard_at(i)
         for kind, p in enumerate((p_own, p_x, p_y, p_d)):
-            landed(s, p, 1 - c, mr.at[s, kind])
+            for j in range(CHUNKS):
+                landed(s, p, 1 - c, j, mr.at[s, kind * CHUNKS + j])
+
+    units = (planes - 1) * CHUNKS
+
+    def step(k):
+        if k < units:
+            i, j = k // CHUNKS + 1, k % CHUNKS
+            stage_z(i, j)
+            if j == CHUNKS - 1:
+                stage_z(i, CHUNKS)
+        if 0 <= k - 2 < units:
+            stage_xy((k - 2) // CHUNKS + 1, (k - 2) % CHUNKS)
+        if 0 <= k - 4 < units:
+            stage_d((k - 4) // CHUNKS + 1, (k - 4) % CHUNKS)
 
     def finish(i):
         s = shard_at(i)
 
         @pl.when((s < z) & (z < planes - 1))
         def _():
-            z_up(s).wait_send()
+            for n in range(CHUNKS + 1):
+                z_up(s, n).wait_send()
 
         @pl.when((s > z) & (z > 0))
         def _():
-            z_dn(s).wait_send()
-
-        x_copy(s).wait_send()
-        y_copy(s).wait_send()
-        d_copy(s).wait_send()
-        for kind in range(4):
-            m_copy(s, kind).wait_send()
+            for n in range(CHUNKS + 1):
+                z_dn(s, n).wait_send()
+
+        for j in range(CHUNKS):
+            x_copy(s, j).wait_send()
+            y_copy(s, j).wait_send()
+            if j > 0:
+                d_copy(s, j).wait_send()
+            for kind in range(4):
+                m_copy(s, kind, j).wait_send()
 
     loads[0].wait()
     loads[1].wait()
@@ -304,6 +340,7 @@
     ]
     for copy in mate_sums:
         copy.start()
+    step(0)
     diagonal = (
         lax.broadcasted_iota(jnp.int32, (HD, HD), 0) == lax.broadcasted_iota(jnp.int32, (HD, HD), 1)
     ).astype(F32)
@@ -316,7 +353,7 @@
     x_sum = remote(x_out, x_in, qs, qr, xn)
     x_sum.start()
     own[...] = part[r] + mate_in[x].astype(F32)
-    stage_z(1)
+    step(1)
     x_sum.wait_recv()
 
     @pl.when(z == 0)
@@ -330,8 +367,8 @@
     upper = z * 2 >= planes
 
     def early():
-        stage_xy(1)
-        stage_z(2)
+        step(2)
+        step(3)
 
     pl.when(upper)(early)
 
@@ -371,15 +408,15 @@
     read_x.start()
     read_mate.start()
     pl.when(jnp.logical_not(upper))(early)
+    step(4)
 
     def got(group, sem):
         pltpu.make_async_copy(reads.at[group], reads.at[group], sem).wait()
 
     got(other_x, gr.at[1])
     relay.start()
-    stage_d(1)
-    stage_xy(2)
-    stage_z(3) if planes > 3 else None
+    step(5)
+    step(6)
     got(2 * x + 1 - c, gr.at[0])
     got(2 * (1 - x) + 1 - c, gr.at[2])
     loads[2].wait()
@@ -399,49 +436,59 @@
         return carry
 
     lax.fori_loop(0, frames, read_step, 0)
-    for i in range(4, planes):
-        stage_z(i)
-    for i in range(3, planes):
-        stage_xy(i)
-    for i in range(2, planes):
-        stage_d(i)
-    for i in range(1, planes):
-        stage_m(i)
-    loads[3].wait()
-
     def product(s, lanes):
         return lax.dot_general(
             wv[s, :depth, lanes], normed[s], (((0,), (0,)), ((), ())), preferred_element_type=F32
         )
 
-    def project(lanes):
-        total = product(0, lanes)
-        for s in range(1, planes):
-            total += product(s, lanes)
-        for f in range(frames):
-            for row in range(lat_rows):
-                at = (f * lat_rows + row) * lat_cols
-                out_ref[f, row, lanes, :] = total[:, at : at + lat_cols].astype(BF16)
+    def project(turn, lanes):
+        s = z if turn == 0 else shard_at(turn)
+        add = product(s, lanes)
+        if turn > 0:
+            add = acc[lanes, :] + add
+        if turn < planes - 1:
+            acc[lanes, :] = add
+        else:
+            for f in range(frames):
+                for row in range(lat_rows):
+                    at = (f * lat_rows + row) * lat_cols
+                    out_ref[f, row, lanes, :] = add[:, at : at + lat_cols].astype(BF16)
 
     tile = 256
 
-    def project_step(n, carry):
-        project(pl.ds(pl.multiple_of(n * tile, tile), tile))
-        return carry
-
-    lax.fori_loop(0, width // tile, project_step, 0)
-    if width % tile:
-        project(slice(width // tile * tile, width))
+    def project_all(turn):
+        def project_step(n, carry):
+            project(turn, pl.ds(pl.multiple_of(n * tile, tile), tile))
+            return carry
+
+        lax.fori_loop(0, width // tile, project_step, 0)
+        if width % tile:
+            project(turn, slice(width // tile * tile, width))
+
+    step(7)
+    step(8)
+    loads[3].wait()
+    project_all(0)
+    done = 8
+    for turn in range(1, planes):
+        last = turn * CHUNKS + 3 + (1 if turn < planes - 1 else 0)
+        for k in range(done + 1, last + 1):
+            step(k)
+        done = max(done, last)
+        stage_m(turn)
+        project_all(turn)
 
     @pl.when(z < planes - 1)
     def _():
-        first_up().wait_send()
+        for n in range(CHUNKS + 1):
+            first_up(n).wait_send()
         for h in range(per):
             chain_copy(h).wait_send()
 
     @pl.when(z > 0)
     def _():
-        first_dn().wait_send()
+        for n in range(CHUNKS + 1):
+            first_dn(n).wait_send()
 
     for i in range(1, planes):
         finish(i)
@@ -458,7 +505,7 @@
     planes, groups = mesh_shape["frm"], mesh_shape["row"]
     per = HEADS // groups
     depth = out_weight.shape[0]
-    rows, cols = round_up(depth, 64), round_up(width, 256)
+    rows, cols = round_up(depth, 64 * CHUNKS), round_up(width, 256)
     weight = jnp.pad(out_weight, ((0, rows - depth), (0, cols - width)))
     dma = pltpu.SemaphoreType.DMA
     shape = (frames, lat_rows, width, lat_cols)
@@ -488,10 +535,12 @@
             pltpu.VMEM((groups,) + per_group, BF16),
             pltpu.VMEM((planes, depth, frames * lat_rows * lat_cols), BF16),
             pltpu.VMEM((width, 1), F32),
+            pltpu.VMEM((width, frames * lat_rows * lat_cols), F32),
             dma((4,)),
         ]
-        + [dma((planes,))] * 9
-        + [dma((planes, 4))] * 2
+        + [dma((planes, CHUNKS + 1))] * 3
+        + [dma((planes, CHUNKS))] * 6
+        + [dma((planes, 4 * CHUNKS))] * 2
         + [dma((groups // 2,))] * 2
         + [dma(()), dma(())]
         + [dma((per,))] * 2

time: 87.6 us -> 79.7 us (0.910)
  the two profiles are of different devices: /device:TPU:25 before, /device:TPU:0 now
where the time goes in v3:
time: 79.7 us; the launch traced here: 79.4 us
  Pallas kernels  71.4 us (90%)
  local copies, waits for them, and re-layouts  7.93 us (10%)
    pallas_call x1, Pallas kernels, local_fused(): pl.pallas_call(functools.partial(fused, planes, 'grp', 'frm', 'row'), out...  71.4 us
    pad x1, local copies, waits for them, and re-layouts, local_fused(): weight = jnp.pad(out_weight, ((0, rows - depth), (0, cols - width)))  3.44 us
    unnamed x1, local copies, waits for them, and re-layouts  3.18 us

profile of v3, /device:TPU:0, one launch (start us, length us, event | category | flops | bytes accessed | tf_op | source)
XLA Modules:
  0.0 79.4 jit_solution(12710830935572762843)
XLA Ops:
  0.0 1.3 %reshape.3.gain_ref = f32[1,2240]{1,0:T(1,128)} reshape(f32[2240]{0:T(1024)} %param.13) | data formatting | bytes 17920 | tf_op jit(solution)/shard_map/reshape | solution.py:553
  1.3 3.4 %pad.4.w_hbm = bf16[576,2304]{1,0:T(8,128)(2,1)} pad(bf16[560,2240]{1,0:T(8,128)(2,1)} %param.12, bf16[]{:T(256)} %constant.2.clone.1), padding=0_16x0_64 | pad | bytes 5163010 | tf_op jit(solution)/shard_map/jit(_pad)/pad | solution.py:509
  4.7 71.4 %shard_map.73 = bf16[2,2,2240,128]{3,2,1,0:T(8,128)(2,1)} custom-call(bf16[2,2,2240,128]{3,2,1,0:T(8,128)(2,1)} %bitcast.5, bf16[2,2,2240,128]{3,2,1,0:T(8,128)(2,1)} %bitcast.6, bf16[2,2,2240,128]{3,2,1,0:T(8,128)(2,1)} %bitcast.7, bf16[576,2304]{1,0:T(8,128)(2,1)} %pad.4.w_hbm, f32[1,2240]{1,0:T(1,128)} %reshape.3.gain_ref, s32[2]{0:T(128)} %flag_ref.1, ...), custom_call_target="tpu_custom_call" | custom-call | tf_op jit(solution)/shard_map/pallas_call | solution.py:517
  76.2 3.2 %copy.9 = bf16[2,2,128,2240]{2,3,1,0:T(8,128)(2,1)} copy(bf16[2,2,128,2240]{2,3,1,0:T(8,128)(2,1)} %bitcast.4) | data formatting | bytes 4587520

commit v4 on v3

--- a/solution.py
+++ b/solution.py
@@ -125,7 +125,7 @@
 def fused(
     planes, grp_axis, frm_axis, row_axis,
     q_hbm, k_hbm, v_hbm, w_hbm, gain_ref, flag_ref, block_ref, out_ref,
-    qv, kv, vv, wv, part, sent, mate_in, x_out, x_in, own, chain_in, chain_out, reads, normed, gains, acc,
+    qv, kv, vv, wl, wv, part, sent, mate_in, x_out, x_in, own, chain_in, chain_out, reads, normed, gains, acc,
     load_sem, zs_up, zs_dn, zr, xs, xr, ys, yr, ds, dr, ms, mr,
     ps, pr, qs, qr, cs, cr, gs, gr,
 ):
@@ -176,10 +176,12 @@
         pltpu.make_async_copy(k_hbm, kv, load_sem.at[0]),
         pltpu.make_async_copy(v_hbm, vv, load_sem.at[1]),
         pltpu.make_async_copy(q_hbm, qv, load_sem.at[2]),
-        pltpu.make_async_copy(w_hbm, wv.at[z], load_sem.at[3]),
+        pltpu.make_async_copy(w_hbm, wl, load_sem.at[3]),
     ]
-    for load in loads:
+    for load in reversed(loads):
         load.start()
+    loads[3].wait()
+    wv[z, :depth, :width] = wl[...]
     inner = (z > 0) & (z < planes - 1)
 
     @pl.when(inner)
@@ -194,11 +196,11 @@
 
     def first_up(n):
         p, j = along[n]
-        return remote(w_hbm.at[cut(p, c, j)], piece(z, p, c, j), zs_up.at[z, n], zr.at[z, n], up)
+        return remote(piece(z, p, c, j), piece(z, p, c, j), zs_up.at[z, n], zr.at[z, n], up)
 
     def first_dn(n):
         p, j = along[n]
-        return remote(w_hbm.at[cut(p, c, j)], piece(z, p, c, j), zs_dn.at[z, n], zr.at[z, n], dn)
+        return remote(piece(z, p, c, j), piece(z, p, c, j), zs_dn.at[z, n], zr.at[z, n], dn)
 
     for n in range(CHUNKS + 1):
 
@@ -289,10 +291,10 @@
             stage_z(i, j)
             if j == CHUNKS - 1:
                 stage_z(i, CHUNKS)
-        if 0 <= k - 2 < units:
-            stage_xy((k - 2) // CHUNKS + 1, (k - 2) % CHUNKS)
-        if 0 <= k - 4 < units:
-            stage_d((k - 4) // CHUNKS + 1, (k - 4) % CHUNKS)
+        if 0 <= k - 3 < units:
+            stage_xy((k - 3) // CHUNKS + 1, (k - 3) % CHUNKS)
+        if 0 <= k - 6 < units:
+            stage_d((k - 6) // CHUNKS + 1, (k - 6) % CHUNKS)
 
     def finish(i):
         s = shard_at(i)
@@ -344,9 +346,10 @@
     diagonal = (
         lax.broadcasted_iota(jnp.int32, (HD, HD), 0) == lax.broadcasted_iota(jnp.int32, (HD, HD), 1)
     ).astype(F32)
+    gain = gain_ref[...].reshape(1, width)
     for h in range(groups * per):
         span = slice(h * HD, (h + 1) * HD)
-        gains[span, :] = jnp.sum(diagonal * gain_ref[:, span], axis=1, keepdims=True)
+        gains[span, :] = jnp.sum(diagonal * gain[:, span], axis=1, keepdims=True)
     for copy in mate_sums:
         copy.wait_recv()
     x_out[...] = (part[2 * (1 - x) + c] + mate_in[1 - x].astype(F32)).astype(BF16)
@@ -467,11 +470,10 @@
 
     step(7)
     step(8)
-    loads[3].wait()
     project_all(0)
     done = 8
     for turn in range(1, planes):
-        last = turn * CHUNKS + 3 + (1 if turn < planes - 1 else 0)
+        last = turn * CHUNKS + 5 + (1 if turn < planes - 1 else 0)
         for k in range(done + 1, last + 1):
             step(k)
         done = max(done, last)
@@ -506,7 +508,6 @@
     per = HEADS // groups
     depth = out_weight.shape[0]
     rows, cols = round_up(depth, 64 * CHUNKS), round_up(width, 256)
-    weight = jnp.pad(out_weight, ((0, rows - depth), (0, cols - width)))
     dma = pltpu.SemaphoreType.DMA
     shape = (frames, lat_rows, width, lat_cols)
     anywhere = pl.BlockSpec(memory_space=pl.ANY)
@@ -523,6 +524,7 @@
             pltpu.VMEM(shape, BF16),
             pltpu.VMEM(shape, BF16),
             pltpu.VMEM(shape, BF16),
+            pltpu.VMEM(out_weight.shape, BF16),
             pltpu.VMEM((planes, rows, cols), BF16),
             pltpu.VMEM((groups,) + per_group, F32),
             pltpu.VMEM((groups,) + per_group, BF16),
@@ -549,8 +551,8 @@
             collective_id=0, has_side_effects=True, vmem_limit_bytes=56 * 1024 * 1024
         ),
     )(
-        *(jnp.swapaxes(a, 2, 3) for a in (queries, keys, values)), weight,
-        norm_gain.reshape(1, width), flags, blocks,
+        *(jnp.swapaxes(a, 2, 3) for a in (queries, keys, values)), out_weight,
+        norm_gain, flags, blocks,
     )
     return jnp.swapaxes(out, 2, 3)
 

time: 79.7 us -> 74.1 us (0.930)
  the two profiles are of different devices: /device:TPU:0 before, /device:TPU:25 now
where the time goes in v4:
time: 74.1 us; the launch traced here: 73.4 us
  Pallas kernels  70.2 us (95%)
  local copies, waits for them, and re-layouts  3.18 us (4%)
    pallas_call x1, Pallas kernels, local_fused(): pl.pallas_call(functools.partial(fused, planes, 'grp', 'frm', 'row'), out...  70.2 us
    unnamed x1, local copies, waits for them, and re-layouts  3.18 us

profile of v4, /device:TPU:25, one launch (start us, length us, event | category | flops | bytes accessed | tf_op | source)
XLA Modules:
  0.0 73.4 jit_solution(2464984529896463598)
XLA Ops:
  0.0 70.2 %shard_map.73 = bf16[2,2,2240,128]{3,2,1,0:T(8,128)(2,1)} custom-call(bf16[2,2,2240,128]{3,2,1,0:T(8,128)(2,1)} %bitcast.5, bf16[2,2,2240,128]{3,2,1,0:T(8,128)(2,1)} %bitcast.6, bf16[2,2,2240,128]{3,2,1,0:T(8,128)(2,1)} %bitcast.7, bf16[560,2240]{1,0:T(8,128)(2,1)} %w_hbm.1, f32[2240]{0:T(1024)} %gain_ref.1, s32[2]{0:T(128)} %flag_ref.1, s32[2]{0:T(128)} %block_ref.1), custom_call_target="tpu_custom_call" | custom-call | tf_op jit(solution)/shard_map/pallas_call | solution.py:518
  70.2 3.2 %copy.9 = bf16[2,2,128,2240]{2,3,1,0:T(8,128)(2,1)} copy(bf16[2,2,128,2240]{2,3,1,0:T(8,128)(2,1)} %bitcast.4) | data formatting | bytes 4587520

commit v5 on v4

--- a/solution.py
+++ b/solution.py
@@ -474,6 +474,7 @@
     done = 8
     for turn in range(1, planes):
         last = turn * CHUNKS + 5 + (1 if turn < planes - 1 else 0)
+        last = max(last, units + 2)
         for k in range(done + 1, last + 1):
             step(k)
         done = max(done, last)

time: 74.1 us -> 77.2 us (1.042)
  Pallas kernels: 70.2 us -> 73.2 us
    pallas_call x1, Pallas kernels: 70.2 us -> 73.2 us  [local_fused(): pl.pallas_call(functools.partial(fused, planes, 'grp', 'frm', 'row'), out...]
where the time goes in v5:
time: 77.2 us; the launch traced here: 76.4 us
  Pallas kernels  73.2 us (95%)
  local copies, waits for them, and re-layouts  3.18 us (4%)
    pallas_call x1, Pallas kernels, local_fused(): pl.pallas_call(functools.partial(fused, planes, 'grp', 'frm', 'row'), out...  73.2 us
    unnamed x1, local copies, waits for them, and re-layouts  3.18 us

profile of v5, /device:TPU:25, one launch (start us, length us, event | category | flops | bytes accessed | tf_op | source)
XLA Modules:
  0.0 76.4 jit_solution(167972329166525861)
XLA Ops:
  0.0 73.2 %shard_map.73 = bf16[2,2,2240,128]{3,2,1,0:T(8,128)(2,1)} custom-call(bf16[2,2,2240,128]{3,2,1,0:T(8,128)(2,1)} %bitcast.5, bf16[2,2,2240,128]{3,2,1,0:T(8,128)(2,1)} %bitcast.6, bf16[2,2,2240,128]{3,2,1,0:T(8,128)(2,1)} %bitcast.7, bf16[560,2240]{1,0:T(8,128)(2,1)} %w_hbm.1, f32[2240]{0:T(1024)} %gain_ref.1, s32[2]{0:T(128)} %flag_ref.1, s32[2]{0:T(128)} %block_ref.1), custom_call_target="tpu_custom_call" | custom-call | tf_op jit(solution)/shard_map/pallas_call | solution.py:519
  73.2 3.2 %copy.9 = bf16[2,2,128,2240]{2,3,1,0:T(8,128)(2,1)} copy(bf16[2,2,128,2240]{2,3,1,0:T(8,128)(2,1)} %bitcast.4) | data formatting | bytes 4587520
